TPU v7x, 32 devices: a whole 2x2x4 slice. The times are simulated.
32 devices in a mesh: cell: 8 (over z, y), gene: 4 (over x, core).
Axes of the slice: x: 2, y: 2, z: 4, core: 2. Of those that a mesh axis runs over, the one named last changes fastest.
Arguments:
- expression: bfloat16 [65536, 512], P('cell', 'gene'), may hold values from 0 to 9, as said below
- affinity: bfloat16 [448, 256, 256], P('cell', 'gene'), may hold values from 0 to 1, as said below
- tile_rows: int32 [448], P('cell'), may hold values from 0 to 255, as said below
- tile_cols: int32 [448], P('cell'), may hold values from 0 to 255, as said below
- tile_count: int32 [8], P('cell'), may hold values from 35 to 53, as said below
Outputs:
- imputed: float32 [65536, 512], P('cell', 'gene')
Inputs may be any that keep to these rules, and one draw needn't show every extreme that they name: `tile_rows`: the slots of index d of cell hold row blocks d * 32 to (d + 1) * 32 - 1. Among its first tile_count[d] slots each of those row blocks appears exactly once with itself as column block, and every other such slot names a column block of another index of cell. `tile_cols`: among the slots in use of one index of cell at most 3 name column blocks of any one other index, and on every index exactly 3 name those of some other index. A pair of blocks may repeat. `tile_count`: both ends are reached in every draw. `expression`: Positive. `affinity`: Positive.
All inputs are finite; a program needn't handle non-finite values.
Results may differ from a plain program's by a relative error of at most 0.0027.
Values may be sent and summed in bfloat16 or wider, within the bound.
A program may use at most 192 MiB of HBM per device.

v0:
```python
import jax
import jax.numpy as jnp
from jax import lax
from jax.sharding import PartitionSpec as P

BS = 256
BLK_DEV = 32
REQ_CAP = 3
STEPS = 3


def ranks_of(owner, remote):
    count = owner.shape[-1]
    order = jnp.arange(count, dtype=jnp.int32)
    earlier = order[None, :] < order[:, None]
    same = (owner[..., :, None] == owner[..., None, :]) & remote[..., None, :] & earlier
    return jnp.sum(same.astype(jnp.int32), axis=-1)


def accumulate(tile_part, pool_part, source, row_index):
    operand = pool_part[source]
    product = jnp.einsum("tij,tjg->tig", tile_part, operand, preferred_element_type=jnp.float32)
    return jax.ops.segment_sum(product, row_index, BLK_DEV)


def on_device(expression, affinity, tile_rows, tile_cols, tile_count):
    me = lax.axis_index("cell")
    peers = lax.axis_size("cell")
    genes = expression.shape[1]
    tiles = lax.all_gather(affinity, "gene", axis=1, tiled=True)
    slots = tiles.shape[0]
    order = jnp.arange(slots, dtype=jnp.int32)
    valid = order < tile_count[0]
    local_row = tile_rows - me * BLK_DEV
    row_index = jnp.where(valid, local_row, 0)
    owner = tile_cols // BLK_DEV
    col_slot = tile_cols - owner * BLK_DEV
    eye = jnp.eye(BS, dtype=bool)
    selfish = (tile_rows == tile_cols)[:, None, None] & eye[None]
    keep = valid[:, None, None] & jnp.logical_not(selfish)
    tiles = jnp.where(keep, tiles, jnp.zeros_like(tiles))
    sums = jnp.sum(tiles, axis=-1, dtype=jnp.float32)
    degree = jax.ops.segment_sum(sums, row_index, BLK_DEV)
    remote = valid & (owner != me)
    rank = ranks_of(owner, remote)
    peer_ids = jnp.arange(peers, dtype=jnp.int32)
    place = jnp.arange(REQ_CAP, dtype=jnp.int32)
    hit = (
        remote[:, None, None]
        & (owner[:, None, None] == peer_ids[None, :, None])
        & (rank[:, None, None] == place[None, None, :])
    )
    wanted = jnp.sum(jnp.where(hit, col_slot[:, None, None] + 1, 0), axis=0) - 1
    asked = lax.all_to_all(wanted, "cell", split_axis=0, concat_axis=0, tiled=True)
    source = jnp.where(remote, BLK_DEV + owner * REQ_CAP + rank, jnp.where(valid, col_slot, 0))
    current = expression.reshape(BLK_DEV, BS, genes)
    for step in range(STEPS):
        outgoing = current[jnp.maximum(asked, 0)]
        outgoing = jnp.where((asked >= 0)[:, :, None, None], outgoing, jnp.zeros_like(outgoing))
        incoming = lax.all_to_all(outgoing, "cell", split_axis=0, concat_axis=0, tiled=True)
        pool = jnp.concatenate([current, incoming.reshape(peers * REQ_CAP, BS, genes)], axis=0)
        total = accumulate(tiles, pool, source, row_index)
        smoothed = total / degree[:, :, None]
        if step == STEPS - 1:
            current = smoothed
        else:
            current = smoothed.astype(jnp.bfloat16)
    last = current.reshape(BLK_DEV * BS, genes)
    top_start = jnp.max(expression.astype(jnp.float32), axis=0)
    top_end = jnp.max(last, axis=0)
    top_start, top_end = lax.pmax((top_start, top_end), "cell")
    return last * (top_start / top_end)[None, :]


def solution(mesh):
    return jax.shard_map(
        on_device,
        mesh=mesh,
        in_specs=(P("cell", "gene"), P("cell", "gene", None), P("cell"), P("cell"), P("cell")),
        out_specs=P("cell", "gene"),
        check_vma=False,
    )
```

profile of v0, /device:TPU:0, one launch (start us, length us, event | category | flops | bytes accessed | tf_op | source)
XLA Modules:
  0.0 327.7 jit_solution(72596154458695274)
XLA Ops:
  6.5 0.0 all-gather.2.cloned.1.call-start
  6.5 0.7 all-gather.2.cloned.1.call-update
  7.9 0.7 compare_and_fusion
  8.6 0.2 convert_reduce_fusion.1
  8.8 0.7 compare_select_fusion
  9.5 0.1 select_reduce_fusion
  9.6 0.1 copy.13
  9.7 13.5 %all_to_all.21 = s32[8,1,3]{2,1,0:T(1,128)S(1)} all-to-all(s32[8,1,3]{2,1,0:T(1,128)S(1)} %copy.13), channel_id=1, replica_groups=mesh['cell'=8,'gene'=4] {'cell'}, dimensions={0} | all-to-all | bytes 192 | tf_op jit(solution)/shard_map/all_to_all | solution.py:54
  23.3 0.1 reshape.136
  23.4 0.1 copy.14
  23.5 0.1 copy.15
  23.6 3.6 %gather_fusion = bf16[24,256,128]{2,1,0:T(8,128)(2,1)} fusion(bf16[32,256,128]{2,1,0:T(8,128)(2,1)} %bitcast.22, s32[1024]{0:T(1024)S(1)} %pad_clamp_fusion.1), kind=kCustom, calls=%fused_computation | custom fusion | bytes 3145824 | tf_op jit(solution)/shard_map/gather | solution.py:58
  27.1 0.0 copy-start.2
  27.1 0.0 copy-start
  27.1 2.9 broadcast_select_fusion.2
  30.0 4.3 %all-to-all-start.1 = ((bf16[8,3,256,128]{3,2,1,0:T(8,128)(2,1)}), bf16[8,3,256,128]{3,2,1,0:T(8,128)(2,1)}, u32[]{:S(2)}, u32[]{:S(2)}) async-start(bf16[8,3,256,128]{3,2,1,0:T(8,128)(2,1)} %broadcast_select_fusion.2), calls=%async_computation.1 | async-start | bytes 3145728 | tf_op jit(solution)/shard_map/all_to_all | solution.py:60
  34.3 0.0 copy-done.2
  34.4 36.2 %all-to-all-done.1 = bf16[8,3,256,128]{3,2,1,0:T(8,128)(2,1)} async-done(((bf16[8,3,256,128]{3,2,1,0:T(8,128)(2,1)}), bf16[8,3,256,128]{3,2,1,0:T(8,128)(2,1)}, u32[]{:S(2)}, u32[]{:S(2)}) %all-to-all-start.1) | async-done | bytes 1572896 | tf_op jit(solution)/shard_map/all_to_all | solution.py:60
  70.5 0.0 copy-done
  70.5 3.6 %pad_maximum_fusion = bf16[56,256,128]{2,1,0:T(8,128)(2,1)} fusion(bf16[24,256,128]{2,1,0:T(8,128)(2,1)} %bitcast.5, bf16[32,256,128]{2,1,0:T(8,128)(2,1)S(1)} %bitcast.23), kind=kLoop, calls=%fused_computation.15 | loop fusion | flops 1835008 | bytes 7340032 | tf_op jit(solution)/shard_map/concatenate | solution.py:61
  74.1 4.9 %gather_fusion.1 = bf16[56,256,128]{2,1,0:T(8,128)(2,1)} fusion(bf16[56,256,128]{2,1,0:T(8,128)(2,1)} %pad_maximum_fusion, s32[1024]{0:T(1024)S(1)} %pad_clamp_fusion), kind=kCustom, calls=%fused_computation.1 | custom fusion | bytes 7340256 | tf_op jit(solution)/shard_map/gather | solution.py:21
  79.0 0.0 all-gather.2.cloned.1.call-done
  79.0 0.0 copy-start.1
  79.0 10.1 %convert_reduce_fusion = (f32[56,256]{1,0:T(8,128)S(1)}, bf16[56,256,256]{2,1,0:T(8,128)(2,1)}) fusion(bf16[56,256,256]{2,1,0:T(8,128)(2,1)} %all-gather.2.cloned.1.call-done, pred[256,256]{1,0:T(8,128)(4,1)S(1)} %iota_compare_fusion, pred[56]{0:T(512)(128)(4,1)S(1)} %get-tuple-element.15, pred[56]{0:T(512)(128)(4,1)S(1)} %get-tuple-element.16), kind=kLoop, calls=%fused_computation.10 | loop fusion | flops 22005760 | bytes 14803056 | tf_op jit(solution)/shard_map/reduce_sum | solution.py:42
  89.1 0.0 copy-done.1
  89.1 8.2 %fusion.5 = f32[56,256,128]{2,1,0:T(8,128)} fusion(bf16[56,256,256]{2,1,0:T(8,128)(2,1)} %get-tuple-element.10, bf16[56,256,128]{2,1,0:T(8,128)(2,1)S(1)} %copy-done.1), kind=kOutput, calls=%fused_computation.48 | convolution fusion | flops 939524096 | bytes 18350080 | tf_op jit(solution)/shard_map/tij,tjg->tig/dot_general | solution.py:22
  97.3 0.9 scatter_custom_fusion.1
  98.2 2.5 broadcast.108.clone.1
  100.7 19.2 %scatter_fusion = f32[32,256,128]{2,1,0:T(8,128)} fusion(f32[32,256,128]{2,1,0:T(8,128)} %broadcast.108.clone.1, s32[56]{0:T(128)S(1)} %subtract_select_fusion, f32[56,256,128]{2,1,0:T(8,128)} %fusion.5), kind=kCustom, calls=%fused_computation.6 | custom fusion | flops 1835008 | bytes 22020320 | tf_op jit(solution)/shard_map/scatter-add | solution.py:23
  119.9 2.9 divide_convert_fusion.1
  122.8 1.9 gather_fusion.2
  124.7 1.6 broadcast_select_fusion.1
  126.3 40.7 %all_to_all.22 = bf16[8,3,256,128]{3,2,1,0:T(8,128)(2,1)S(1)} all-to-all(bf16[8,3,256,128]{3,2,1,0:T(8,128)(2,1)S(1)} %broadcast_select_fusion.1), channel_id=1, replica_groups=mesh['cell'=8,'gene'=4] {'cell'}, dimensions={0} | all-to-all | bytes 3145728 | tf_op jit(solution)/shard_map/all_to_all | solution.py:60
  167.0 2.2 pad_maximum_fusion.1
  169.1 4.9 %gather_fusion.3 = bf16[56,256,128]{2,1,0:T(8,128)(2,1)} fusion(bf16[56,256,128]{2,1,0:T(8,128)(2,1)} %pad_maximum_fusion.1, s32[1024]{0:T(1024)S(1)} %pad_clamp_fusion), kind=kCustom, calls=%fused_computation.3 | custom fusion | bytes 7340256 | tf_op jit(solution)/shard_map/gather | solution.py:21
  174.0 9.2 %fusion.6 = f32[56,256,128]{2,1,0:T(8,128)} fusion(bf16[56,256,256]{2,1,0:T(8,128)(2,1)} %get-tuple-element.10, bf16[56,256,128]{2,1,0:T(8,128)(2,1)} %gather_fusion.3), kind=kOutput, calls=%fused_computation.49 | convolution fusion | flops 939524096 | bytes 18350080 | tf_op jit(solution)/shard_map/tij,tjg->tig/dot_general | solution.py:22
  183.2 2.5 broadcast.108.clone
  185.7 19.2 %scatter_fusion.1 = f32[32,256,128]{2,1,0:T(8,128)} fusion(f32[32,256,128]{2,1,0:T(8,128)} %broadcast.108.clone, s32[56]{0:T(128)S(1)} %subtract_select_fusion, f32[56,256,128]{2,1,0:T(8,128)} %fusion.6), kind=kCustom, calls=%fused_computation.8 | custom fusion | flops 1835008 | bytes 22020320 | tf_op jit(solution)/shard_map/scatter-add | solution.py:23
  205.0 2.9 divide_convert_fusion
  207.8 1.9 gather_fusion.4
  209.8 2.7 broadcast_select_fusion
  212.5 4.3 %all-to-all-start.3 = ((bf16[8,3,256,128]{3,2,1,0:T(8,128)(2,1)}), bf16[8,3,256,128]{3,2,1,0:T(8,128)(2,1)}, u32[]{:S(2)}, u32[]{:S(2)}) async-start(bf16[8,3,256,128]{3,2,1,0:T(8,128)(2,1)} %broadcast_select_fusion), calls=%async_computation.3 | async-start | bytes 3145728 | tf_op jit(solution)/shard_map/all_to_all | solution.py:60
  216.8 2.7 reduce_max.23
  219.5 33.6 %all-to-all-done.3 = bf16[8,3,256,128]{3,2,1,0:T(8,128)(2,1)} async-done(((bf16[8,3,256,128]{3,2,1,0:T(8,128)(2,1)}), bf16[8,3,256,128]{3,2,1,0:T(8,128)(2,1)}, u32[]{:S(2)}, u32[]{:S(2)}) %all-to-all-start.3) | async-done | bytes 1572896 | tf_op jit(solution)/shard_map/all_to_all | solution.py:60
  253.1 3.6 %pad_maximum_fusion.2 = bf16[56,256,128]{2,1,0:T(8,128)(2,1)} fusion(bf16[24,256,128]{2,1,0:T(8,128)(2,1)} %bitcast.9, bf16[32,256,128]{2,1,0:T(8,128)(2,1)S(1)} %divide_convert_fusion), kind=kLoop, calls=%fused_computation.17 | loop fusion | flops 1835008 | bytes 7340032 | tf_op jit(solution)/shard_map/concatenate | solution.py:61
  256.7 4.9 %gather_fusion.5 = bf16[56,256,128]{2,1,0:T(8,128)(2,1)} fusion(bf16[56,256,128]{2,1,0:T(8,128)(2,1)} %pad_maximum_fusion.2, s32[1024]{0:T(1024)S(1)} %pad_clamp_fusion), kind=kCustom, calls=%fused_computation.5 | custom fusion | bytes 7340256 | tf_op jit(solution)/shard_map/gather | solution.py:21
  261.6 9.2 %fusion.7 = f32[56,256,128]{2,1,0:T(8,128)} fusion(bf16[56,256,256]{2,1,0:T(8,128)(2,1)} %get-tuple-element.10, bf16[56,256,128]{2,1,0:T(8,128)(2,1)} %gather_fusion.5), kind=kOutput, calls=%fused_computation.50 | convolution fusion | flops 939524096 | bytes 18350080 | tf_op jit(solution)/shard_map/tij,tjg->tig/dot_general | solution.py:22
  270.8 2.5 broadcast.108
  273.3 19.2 %scatter_fusion.2 = f32[32,256,128]{2,1,0:T(8,128)} fusion(f32[32,256,128]{2,1,0:T(8,128)} %broadcast.108, s32[56]{0:T(128)S(1)} %subtract_select_fusion, f32[56,256,128]{2,1,0:T(8,128)} %fusion.7), kind=kCustom, calls=%fused_computation.9 | custom fusion | flops 1835008 | bytes 22020320 | tf_op jit(solution)/shard_map/scatter-add | solution.py:23
  292.5 4.1 %fusion.4 = (f32[128]{0:T(128)S(1)}, f32[32,256,128]{2,1,0:T(8,128)}) fusion(f32[32,256,128]{2,1,0:T(8,128)} %scatter_fusion.2, f32[32,256]{1,0:T(8,128)S(1)} %scatter_custom_fusion.1), kind=kLoop, calls=%fused_computation.47 | loop fusion | flops 2097024 | bytes 8421888 | tf_op jit(solution)/shard_map/reduce_max | solution.py:70
  296.6 19.7 %all-reduce = (f32[128]{0:T(128)S(1)}, f32[128]{0:T(128)S(1)}) all-reduce(bf16[128]{0:T(256)(128)(2,1)S(1)} %reduce_max.23, f32[128]{0:T(128)S(1)} %get-tuple-element.7), channel_id=1, replica_groups=mesh['cell'=8,'gene'=4] {'cell'}, use_global_device_ids=true, to_apply=%region_8.9 | all-reduce | flops 256 | bytes 1792 | tf_op jit(solution)/shard_map/pmax | solution.py:71
  316.4 4.5 %bitcast_multiply_fusion = f32[8192,128]{1,0:T(8,128)} fusion(f32[32,256,128]{2,1,0:T(8,128)} %get-tuple-element.8, f32[128]{0:T(128)S(1)} %div.43), kind=kLoop, calls=%fused_computation.12 | loop fusion | flops 1048576 | bytes 8389120 | tf_op jit(solution)/shard_map/mul | solution.py:72
  (10 shorter events, 0.1 us)
Async XLA Ops:
  6.5 72.5 %all-gather.2.cloned.1.call-start = ((), (), s32[]{:S(2)}) async-start(), calls=%async_computation.4 | async-start | bytes 9175040 | tf_op jit(solution)/shard_map/all_gather | solution.py:30
  27.1 7.2 %copy-start.2 = (s32[56]{0:T(128)S(1)}, s32[56]{0:T(128)}, u32[]{:S(2)}) copy-start(s32[56]{0:T(128)} %param.7) | copy-start | bytes 676
  27.1 43.4 %copy-start = (bf16[8192,128]{1,0:T(8,128)(2,1)S(1)}, bf16[8192,128]{1,0:T(8,128)(2,1)}, u32[]{:S(2)}) copy-start(bf16[8192,128]{1,0:T(8,128)(2,1)} %param.5) | copy-start | bytes 6291460
  30.0 40.5 %all-to-all-start.1 = ((bf16[8,3,256,128]{3,2,1,0:T(8,128)(2,1)}), bf16[8,3,256,128]{3,2,1,0:T(8,128)(2,1)}, u32[]{:S(2)}, u32[]{:S(2)}) async-start(bf16[8,3,256,128]{3,2,1,0:T(8,128)(2,1)} %broadcast_select_fusion.2), calls=%async_computation.1 | async-start | bytes 3145728 | tf_op jit(solution)/shard_map/all_to_all | solution.py:60
  79.0 10.1 %copy-start.1 = (bf16[56,256,128]{2,1,0:T(8,128)(2,1)S(1)}, bf16[56,256,128]{2,1,0:T(8,128)(2,1)}, u32[]{:S(2)}) copy-start(bf16[56,256,128]{2,1,0:T(8,128)(2,1)} %gather_fusion.1) | copy-start | bytes 11010052
  212.5 40.6 %all-to-all-start.3 = ((bf16[8,3,256,128]{3,2,1,0:T(8,128)(2,1)}), bf16[8,3,256,128]{3,2,1,0:T(8,128)(2,1)}, u32[]{:S(2)}, u32[]{:S(2)}) async-start(bf16[8,3,256,128]{3,2,1,0:T(8,128)(2,1)} %broadcast_select_fusion), calls=%async_computation.3 | async-start | bytes 3145728 | tf_op jit(solution)/shard_map/all_to_all | solution.py:60
Sparse Core Ops, SparseCore 0:
  8.9 55.0 all-gather.1
where the time goes:
time: 328 us
  other arithmetic  104 us (32%)
  blocking collectives  73.9 us (23%)
  waiting for transfers between devices  70.5 us (21%)
  local copies, waits for them, and re-layouts  30 us (9%)
  matrix products  26.7 us (8%)
  between operations  14.2 us (4%)
  starting transfers between devices  8.59 us (3%)
    all_to_all x2, waiting for transfers between devices, on_device(): lax.all_to_all(outgoing, 'cell', split_axis=0, concat_axis=0, tiled=True)  69.8 us
    scatter-add x3, other arithmetic, accumulate(): return jax.ops.segment_sum(product, row_index, BLK_DEV)  57.7 us
    all_to_all x1, blocking collectives, on_device(): lax.all_to_all(outgoing, 'cell', split_axis=0, concat_axis=0, tiled=True)  40.7 us
    dot_general x3, matrix products, accumulate(): jnp.einsum('tij,tjg->tig', tile_part, operand, preferred_element_type=jnp...  26.7 us
    pmax x1, blocking collectives, on_device(): top_start, top_end = lax.pmax((top_start, top_end), 'cell')  19.7 us
    gather x3, local copies, waits for them, and re-layouts, accumulate(): operand = pool_part[source]  14.7 us
    all_to_all x1, blocking collectives, on_device(): lax.all_to_all(wanted, 'cell', split_axis=0, concat_axis=0, tiled=True)  13.5 us
    reduce_sum x1, other arithmetic, on_device(): sums = jnp.sum(tiles, axis=-1, dtype=jnp.float32)  10.1 us
  transfers between devices with their start and end apart: 3, of which 2 were waited for; matrix products, arithmetic and copies ran while one was open for 6% of the time, Pallas kernels for 0%

commit v1 on v0

v1 whole, which is shorter than its diff:
```python
import functools
import jax
import jax.numpy as jnp
from jax import lax
from jax.experimental import pallas as pl
from jax.experimental.pallas import tpu as pltpu
from jax.sharding import PartitionSpec as P

BS = 256
BLK_DEV = 32
REQ_CAP = 3
STEPS = 3
MESH = pl.DeviceIdType.MESH


def spans(first, last, size):
    return [(at, min(size, last - at)) for at in range(first, last, size)]


def kernel(
    n, meta, wanted, x_ref, aff, last_hbm, ratio,
    a_full, cur, total, deg, chain, inc, out, asked_v, asked_s, tops, tops_in,
    req_send, req_recv, x_send, x_recv, a_send, a_recv, top_send, top_recv, local_sem, hbm_sem,
):
    far = n - 1
    links = far * REQ_CAP
    slots = BLK_DEV + links
    prev_at = slots
    last_at = slots + links
    chunks = spans(0, BLK_DEV, 8) + spans(BLK_DEV, slots, max(7, links // 4))
    me = lax.axis_index("cell")
    g = lax.axis_index("gene")
    across = lax.rem(g + 2, 4)
    sister = g + 1 - 2 * lax.rem(g, 2)
    rows = aff.shape[1]

    def after(d):
        return lax.rem(me + d, n)

    def before(d):
        return lax.rem(me + n - d, n)

    barrier = pltpu.get_barrier_semaphore()

    def greet(d, carry):
        pl.semaphore_signal(barrier, inc=1, device_id={"cell": after(d)}, device_id_type=MESH)
        return carry

    lax.fori_loop(1, n, greet, 0)
    for other in (across, sister):
        pl.semaphore_signal(barrier, inc=1, device_id={"gene": other}, device_id_type=MESH)
    pl.semaphore_wait(barrier, far + 2)

    def request(d):
        return pltpu.make_async_remote_copy(
            src_ref=wanted.at[d - 1], dst_ref=asked_v.at[d - 1],
            send_sem=req_send.at[d - 1], recv_sem=req_recv.at[d - 1],
            device_id={"cell": before(d)}, device_id_type=MESH,
        )

    def blocks(d, side):
        return pltpu.make_async_remote_copy(
            src_ref=out.at[d - 1], dst_ref=inc.at[side, d - 1],
            send_sem=x_send.at[d - 1], recv_sem=x_recv.at[side, d - 1],
            device_id={"cell": after(d)}, device_id_type=MESH,
        )

    def peak(d):
        return pltpu.make_async_remote_copy(
            src_ref=tops, dst_ref=tops_in.at[d - 1],
            send_sem=top_send.at[d - 1], recv_sem=top_recv.at[d - 1],
            device_id={"cell": after(d)}, device_id_type=MESH,
        )

    def slab(c, kind):
        at, size = chunks[c]
        holder = across if kind == 2 else g
        other = across if kind == 0 else sister
        part = a_full.at[holder, pl.ds(at, size)]
        return pltpu.make_async_remote_copy(
            src_ref=part, dst_ref=part,
            send_sem=a_send.at[c, kind], recv_sem=a_recv.at[c, kind],
            device_id={"gene": other}, device_id_type=MESH,
        )

    def each(function):
        def body(d, carry):
            function(d)
            return carry
        lax.fori_loop(1, n, body, 0)

    each(lambda d: request(d).start())

    line = lax.broadcasted_iota(jnp.int32, (rows, BS), 0) + g * rows
    column = lax.broadcasted_iota(jnp.int32, (rows, BS), 1)
    keep = jnp.where(line == column, 0.0, 1.0).astype(jnp.bfloat16)
    for c, (at, size) in enumerate(chunks):
        def place(t, carry, own=at < BLK_DEV):
            tile = aff[meta[t]]
            if own:
                tile = tile * keep
            a_full[g, t] = tile
            return carry
        lax.fori_loop(at, at + size, place, 0)
        slab(c, 0).start()
        slab(c, 1).start()

    each(lambda d: request(d).wait())
    copy = pltpu.make_async_copy(asked_v, asked_s, local_sem)
    copy.start()
    copy.wait()

    def send_blocks(source, side):
        def body(d):
            for r in range(REQ_CAP):
                out[d - 1, r] = source[asked_s[d - 1, 0, r]]
            blocks(d, side).start()
        each(body)

    send_blocks(x_ref, 0)

    def tile_of(t):
        return a_full[:, t].reshape(BS, BS)

    def by_four(function):
        def body(q, carry):
            for j in range(4):
                function(q * 4 + j)
            return carry
        lax.fori_loop(0, BLK_DEV // 4, body, 0)

    def dot(a, b):
        return jnp.dot(a, b, preferred_element_type=jnp.float32)

    def own_part(source):
        def body(i):
            total[i] = dot(tile_of(i), source[i])
        by_four(body)

    def link(k, product):
        chain[k + 1] = product + chain[meta[prev_at + k]]

    chain[0] = jnp.zeros((BS, x_ref.shape[2]), jnp.float32)
    ones = jnp.ones((BS, x_ref.shape[2]), jnp.bfloat16)

    def highest(i, top):
        block = x_ref[i].astype(jnp.float32)
        return jnp.maximum(top, jnp.max(block.reshape(BS // 8, 8, -1), axis=0))

    zero_top = jnp.full((8, x_ref.shape[2]), -jnp.inf, jnp.float32)
    start = lax.fori_loop(0, BLK_DEV, highest, zero_top)
    tops[0:8] = start

    for c in range(len(chunks)):
        slab(c, 0).wait_recv()
        slab(c, 2).start()
    for c in range(len(chunks)):
        slab(c, 1).wait_recv()
        slab(c, 2).wait_recv()

    own_part(x_ref)

    def degree_links(d):
        for r in range(REQ_CAP):
            k = (d - 1) * REQ_CAP + r
            link(k, dot(tile_of(BLK_DEV + k), ones))

    each(degree_links)

    def degree_own(i):
        deg[i] = dot(tile_of(i), ones) + chain[meta[last_at + i]]

    by_four(degree_own)

    for step in range(STEPS):
        side = step % 2
        if step > 0:
            own_part(cur)

        def far_part(d):
            blocks(d, side).wait_recv()
            for r in range(REQ_CAP):
                k = (d - 1) * REQ_CAP + r
                link(k, dot(tile_of(BLK_DEV + k), inc[side, d - 1, r]))

        each(far_part)
        if step < STEPS - 1:
            def settle(i):
                value = (total[i] + chain[meta[last_at + i]]) / deg[i]
                cur[i] = value.astype(jnp.bfloat16)
            by_four(settle)
            each(lambda d: blocks(d, side).wait_send())
            send_blocks(cur, 1 - side)
        else:
            def finish(q, top):
                for j in range(4):
                    i = q * 4 + j
                    value = (total[i] + chain[meta[last_at + i]]) / deg[i]
                    total[i] = value
                    top = jnp.maximum(top, jnp.max(value.reshape(BS // 8, 8, -1), axis=0))
                pltpu.make_async_copy(
                    total.at[pl.ds(q * 4, 4)], last_hbm.at[pl.ds(q * 4, 4)], hbm_sem.at[q]
                ).start()
                return top
            tops[8:16] = lax.fori_loop(0, BLK_DEV // 4, finish, zero_top)

    each(lambda d: peak(d).start())
    each(lambda d: blocks(d, (STEPS - 1) % 2).wait_send())
    for c in range(len(chunks)):
        for kind in range(3):
            slab(c, kind).wait_send()
    each(lambda d: peak(d).wait())

    def join(d, carry):
        return jnp.maximum(carry, tops_in[d - 1])

    best = lax.fori_loop(1, n, join, tops[...])
    top_start = jnp.max(best[0:8], axis=0, keepdims=True)
    top_end = jnp.max(best[8:16], axis=0, keepdims=True)
    ratio[...] = jnp.broadcast_to(top_start / top_end, ratio.shape)

    def drain(q, carry):
        pltpu.make_async_copy(
            total.at[pl.ds(q * 4, 4)], last_hbm.at[pl.ds(q * 4, 4)], hbm_sem.at[q]
        ).wait()
        return carry

    lax.fori_loop(0, BLK_DEV // 4, drain, 0)


def plan(me, n, tile_rows, tile_cols, tile_count):
    links = (n - 1) * REQ_CAP
    count = tile_rows.shape[0]
    order = jnp.arange(count, dtype=jnp.int32)
    valid = order < tile_count[0]
    owner = tile_cols // BLK_DEV
    col_slot = tile_cols - owner * BLK_DEV
    row = tile_rows - me * BLK_DEV
    remote = valid & (owner != me)
    own = valid & (owner == me)
    same = (owner[:, None] == owner[None, :]) & remote[None, :] & (order[None, :] < order[:, None])
    rank = jnp.sum(same.astype(jnp.int32), axis=1)
    k = jnp.where(remote, (jnp.mod(me - owner, n) - 1) * REQ_CAP + rank, -1)
    linked = (row[:, None] == row[None, :]) & remote[None, :] & (k[None, :] < k[:, None])
    prev = jnp.max(jnp.where(linked, k[None, :] + 1, 0), axis=1)
    hit = k[:, None] == jnp.arange(links, dtype=jnp.int32)[None, :]
    mine = row[:, None] == jnp.arange(BLK_DEV, dtype=jnp.int32)[None, :]
    own_tile = jnp.sum(jnp.where(mine & own[:, None], order[:, None], 0), axis=0)
    last = jnp.max(jnp.where(mine & remote[:, None], k[:, None] + 1, 0), axis=0)
    pick = lambda value: jnp.sum(jnp.where(hit, value[:, None], 0), axis=0)
    meta = jnp.concatenate([own_tile, pick(order), pick(prev), last])
    wanted = jnp.pad(pick(col_slot).reshape(n - 1, 1, REQ_CAP), ((0, 0), (0, 7), (0, 128 - REQ_CAP)))
    return meta, wanted


def on_device(n, expression, affinity, tile_rows, tile_cols, tile_count):
    me = lax.axis_index("cell")
    genes = expression.shape[1]
    far = n - 1
    links = far * REQ_CAP
    slots = BLK_DEV + links
    parts = BS // affinity.shape[1]
    meta, wanted = plan(me, n, tile_rows, tile_cols, tile_count)
    n_chunks = len(spans(0, BLK_DEV, 8)) + len(spans(BLK_DEV, slots, max(7, links // 4)))
    bf16, f32, i32 = jnp.bfloat16, jnp.float32, jnp.int32
    dma = pltpu.SemaphoreType.DMA
    vmem = pl.BlockSpec(memory_space=pltpu.VMEM)
    last, ratio = pl.pallas_call(
        functools.partial(kernel, n),
        out_shape=(
            jax.ShapeDtypeStruct((BLK_DEV, BS, genes), f32),
            jax.ShapeDtypeStruct((8, genes), f32),
        ),
        in_specs=[pl.BlockSpec(memory_space=pltpu.SMEM), vmem, vmem, vmem],
        out_specs=(pl.BlockSpec(memory_space=pl.ANY), vmem),
        scratch_shapes=[
            pltpu.VMEM((parts, slots, affinity.shape[1], BS), bf16),
            pltpu.VMEM((BLK_DEV, BS, genes), bf16),
            pltpu.VMEM((BLK_DEV, BS, genes), f32),
            pltpu.VMEM((BLK_DEV, BS, genes), f32),
            pltpu.VMEM((links + 1, BS, genes), f32),
            pltpu.VMEM((2, far, REQ_CAP, BS, genes), bf16),
            pltpu.VMEM((far, REQ_CAP, BS, genes), bf16),
            pltpu.VMEM((far, 8, 128), i32),
            pltpu.SMEM((far, 8, 128), i32),
            pltpu.VMEM((16, genes), f32),
            pltpu.VMEM((far, 16, genes), f32),
            dma((far,)), dma((far,)), dma((far,)), dma((2, far)),
            dma((n_chunks, 3)), dma((n_chunks, 3)), dma((far,)), dma((far,)),
            dma, dma((BLK_DEV // 4,)),
        ],
        compiler_params=pltpu.CompilerParams(
            collective_id=0, has_side_effects=True, vmem_limit_bytes=(62 if n > 8 else 48) * 2**20
        ),
    )(meta, wanted, expression.reshape(BLK_DEV, BS, genes), affinity)
    return last.reshape(BLK_DEV * BS, genes) * ratio[0:1]


def solution(mesh):
    return jax.shard_map(
        functools.partial(on_device, mesh.shape["cell"]),
        mesh=mesh,
        in_specs=(P("cell", "gene"), P("cell", "gene", None), P("cell"), P("cell"), P("cell")),
        out_specs=P("cell", "gene"),
        check_vma=False,
    )
```

time: 328 us -> 151 us (0.46)
  Pallas kernels: 0 us -> 140 us
  other arithmetic: 104 us -> 6.53 us
  blocking collectives: 73.9 us -> 0 us
  waiting for transfers between devices: 70.5 us -> 0 us
  local copies, waits for them, and re-layouts: 30 us -> 3.18 us
  matrix products: 26.7 us -> 0 us
  between operations: 14.2 us -> 0.69 us
  starting transfers between devices: 8.59 us -> 0 us
    pallas_call x0 -> x1, Pallas kernels: none -> 140 us  [on_device(): pl.pallas_call(functools.partial(kernel, n), out_shape=(jax.ShapeDtypeStr...]
    all_to_all x2 -> x0, waiting for transfers between devices: 69.8 us -> none  [on_device(): lax.all_to_all(outgoing, 'cell', split_axis=0, concat_axis=0, tiled=True)]
    scatter-add x4 -> x0, other arithmetic: 58.6 us -> none  [the longest x3 57.7 us: accumulate(): return jax.ops.segment_sum(product, row_index, BLK_DEV)]
    all_to_all x2 -> x0, blocking collectives: 54.2 us -> none  [the longest x1 40.7 us: on_device(): lax.all_to_all(outgoing, 'cell', split_axis=0, concat_axis=0, tiled=True)]
    dot_general x3 -> x0, matrix products: 26.7 us -> none  [accumulate(): jnp.einsum('tij,tjg->tig', tile_part, operand, preferred_element_type=jnp...]
    gather x6 -> x0, local copies, waits for them, and re-layouts: 22.1 us -> none  [the longest x3 14.7 us: accumulate(): operand = pool_part[source]]
    pmax x1 -> x0, blocking collectives: 19.7 us -> none  [on_device(): top_start, top_end = lax.pmax((top_start, top_end), 'cell')]
    reduce_sum x3, other arithmetic: 10.4 us -> 0.44 us  [the longest x1 0.18 us: plan(): rank = jnp.sum(same.astype(jnp.int32), axis=1)]
  transfers between devices with their start and end apart: 3 -> 0, of which waited for: 2 -> 0; matrix products, arithmetic and copies ran while one was open for 6% -> 0% of each run, Pallas kernels for 0% -> 0%
where the time goes in v1:
time: 151 us; the launch traced here: 150 us
  Pallas kernels  140 us (93%)
  other arithmetic  6.53 us (4%)
  local copies, waits for them, and re-layouts  3.18 us (2%)
    pallas_call x1, Pallas kernels, on_device(): pl.pallas_call(functools.partial(kernel, n), out_shape=(jax.ShapeDtypeStr...  140 us
    mul x1, other arithmetic, on_device(): return last.reshape(BLK_DEV * BS, genes) * ratio[0:1]  4.47 us
    unnamed x4, local copies, waits for them, and re-layouts  3.09 us

profile of v1, /device:TPU:0, one launch (start us, length us, event | category | flops | bytes accessed | tf_op | source)
XLA Modules:
  0.0 150.4 jit_solution(12794187606498656343)
XLA Ops:
  0.7 0.7 multiply_subtract_fusion
  1.3 0.2 convert_reduce_fusion
  1.5 0.7 broadcast_add_fusion
  2.2 0.2 select_reduce_fusion
  2.4 0.1 select_reduce_fusion.2
  2.5 0.1 select_reduce_fusion.3
  2.6 0.1 pad_add_fusion.meta
  2.7 0.1 reshape.27
  2.8 0.0 copy-start
  2.8 1.6 %copy-done = bf16[8192,128]{1,0:T(8,128)(2,1)S(1)} copy-done((bf16[8192,128]{1,0:T(8,128)(2,1)S(1)}, bf16[8192,128]{1,0:T(8,128)(2,1)}, u32[]{:S(2)}) %copy-start) | copy-done | bytes 2097176
  4.4 0.0 copy-start.1
  4.4 1.5 copy-done.1
  5.9 140.0 %shard_map.55 = (f32[32,256,128]{2,1,0:T(8,128)}, f32[8,128]{1,0:T(8,128)S(1)}) custom-call(s32[106]{0:T(128)S(1)} %pad_add_fusion.meta, s32[7,8,128]{2,1,0:T(8,128)S(1)} %pad.4.wanted, bf16[32,256,128]{2,1,0:T(8,128)(2,1)S(1)} %bitcast.8, bf16[56,64,256]{2,1,0:T(8,128)(2,1)S(1)} %copy-done.1), custom_call_target="tpu_custom_call" | custom-call | tf_op jit(solution)/shard_map/pallas_call | solution.py:268
  145.9 4.5 %bitcast_multiply_fusion = f32[8192,128]{1,0:T(8,128)} fusion(f32[32,256,128]{2,1,0:T(8,128)} %get-tuple-element.7, f32[128]{0:T(128)S(1)} %slice_bitcast_fusion), kind=kLoop, calls=%fused_computation | loop fusion | flops 1048576 | bytes 8389120 | tf_op jit(solution)/shard_map/mul | solution.py:296
  (3 shorter events, 0.0 us)
Async XLA Ops:
  2.8 1.6 %copy-start = (bf16[8192,128]{1,0:T(8,128)(2,1)S(1)}, bf16[8192,128]{1,0:T(8,128)(2,1)}, u32[]{:S(2)}) copy-start(bf16[8192,128]{1,0:T(8,128)(2,1)} %param.5) | copy-start | bytes 6291460
  4.4 1.5 copy-start.1

commit v2 on v1

--- a/solution.py
+++ b/solution.py
@@ -17,22 +17,31 @@
     return [(at, min(size, last - at)) for at in range(first, last, size)]
 
 
+def tile_chunks(links):
+    return spans(BLK_DEV, BLK_DEV + links, max(7, links // 4)) + spans(0, BLK_DEV, 4)
+
+
 def kernel(
-    n, meta, wanted, x_ref, aff, last_hbm, ratio,
-    a_full, cur, total, deg, chain, inc, out, asked_v, asked_s, tops, tops_in,
-    req_send, req_recv, x_send, x_recv, a_send, a_recv, top_send, top_recv, local_sem, hbm_sem,
+    n, meta, wanted, x_hbm, aff_hbm, last_hbm, ratio,
+    a_full, aff, cur, total, deg, chain, inc, out, asked_v, asked_s, tops, tops_in,
+    req_send, req_recv, x_send, x_recv, a_send, a_recv, top_send, top_recv, local_sem, load_sem, hbm_sem,
 ):
     far = n - 1
     links = far * REQ_CAP
     slots = BLK_DEV + links
     prev_at = slots
     last_at = slots + links
-    chunks = spans(0, BLK_DEV, 8) + spans(BLK_DEV, slots, max(7, links // 4))
+    chunks = tile_chunks(links)
     me = lax.axis_index("cell")
     g = lax.axis_index("gene")
     across = lax.rem(g + 2, 4)
     sister = g + 1 - 2 * lax.rem(g, 2)
     rows = aff.shape[1]
+    genes = cur.shape[2]
+    load_aff = pltpu.make_async_copy(aff_hbm, aff, load_sem.at[0])
+    load_aff.start()
+    load_x = pltpu.make_async_copy(x_hbm, cur, load_sem.at[1])
+    load_x.start()
 
     def after(d):
         return lax.rem(me + d, n)
@@ -89,7 +98,21 @@
             return carry
         lax.fori_loop(1, n, body, 0)
 
+    def far_first(function):
+        def body(j, carry):
+            function(n // 2 + ((j + 1) // 2) * (1 - 2 * lax.rem(j, 2)))
+            return carry
+        lax.fori_loop(0, far, body, 0)
+
+    def near_first(function):
+        def body(q, carry):
+            j = far - 1 - q
+            function(q, n // 2 + ((j + 1) // 2) * (1 - 2 * lax.rem(j, 2)))
+            return carry
+        lax.fori_loop(0, far, body, 0)
+
     each(lambda d: request(d).start())
+    load_aff.wait()
 
     line = lax.broadcasted_iota(jnp.int32, (rows, BS), 0) + g * rows
     column = lax.broadcasted_iota(jnp.int32, (rows, BS), 1)
@@ -109,15 +132,16 @@
     copy = pltpu.make_async_copy(asked_v, asked_s, local_sem)
     copy.start()
     copy.wait()
+    load_x.wait()
 
     def send_blocks(source, side):
         def body(d):
             for r in range(REQ_CAP):
                 out[d - 1, r] = source[asked_s[d - 1, 0, r]]
             blocks(d, side).start()
-        each(body)
-
-    send_blocks(x_ref, 0)
+        far_first(body)
+
+    send_blocks(cur, 0)
 
     def tile_of(t):
         return a_full[:, t].reshape(BS, BS)
@@ -132,61 +156,66 @@
     def dot(a, b):
         return jnp.dot(a, b, preferred_element_type=jnp.float32)
 
-    def own_part(source):
+    def own_part():
         def body(i):
-            total[i] = dot(tile_of(i), source[i])
+            total[i] = dot(tile_of(i), cur[i])
         by_four(body)
 
     def link(k, product):
         chain[k + 1] = product + chain[meta[prev_at + k]]
 
-    chain[0] = jnp.zeros((BS, x_ref.shape[2]), jnp.float32)
-    ones = jnp.ones((BS, x_ref.shape[2]), jnp.bfloat16)
+    chain[0] = jnp.zeros((BS, genes), jnp.float32)
+    ones = jnp.ones((BS, genes), jnp.bfloat16)
 
     def highest(i, top):
-        block = x_ref[i].astype(jnp.float32)
+        block = cur[i].astype(jnp.float32)
         return jnp.maximum(top, jnp.max(block.reshape(BS // 8, 8, -1), axis=0))
 
-    zero_top = jnp.full((8, x_ref.shape[2]), -jnp.inf, jnp.float32)
+    zero_top = jnp.full((8, genes), -jnp.inf, jnp.float32)
     start = lax.fori_loop(0, BLK_DEV, highest, zero_top)
     tops[0:8] = start
+
+    def far_degree(k):
+        link(k, dot(tile_of(BLK_DEV + k), ones))
+
+    def own_first(i):
+        both = dot(tile_of(i), jnp.concatenate([cur[i], ones], axis=1))
+        total[i] = both[:, :genes]
+        deg[i] = 1.0 / (both[:, genes:] + chain[meta[last_at + i]])
+
+    def use(c):
+        at, size = chunks[c]
+        slab(c, 1).wait_recv()
+        slab(c, 2).wait_recv()
+        if at >= BLK_DEV:
+            for t in range(at, at + size):
+                far_degree(t - BLK_DEV)
+        else:
+            for t in range(at, at + size):
+                own_first(t)
 
     for c in range(len(chunks)):
         slab(c, 0).wait_recv()
         slab(c, 2).start()
-    for c in range(len(chunks)):
-        slab(c, 1).wait_recv()
-        slab(c, 2).wait_recv()
-
-    own_part(x_ref)
-
-    def degree_links(d):
-        for r in range(REQ_CAP):
-            k = (d - 1) * REQ_CAP + r
-            link(k, dot(tile_of(BLK_DEV + k), ones))
-
-    each(degree_links)
-
-    def degree_own(i):
-        deg[i] = dot(tile_of(i), ones) + chain[meta[last_at + i]]
-
-    by_four(degree_own)
+        if c > 0:
+            use(c - 1)
+    use(len(chunks) - 1)
 
     for step in range(STEPS):
         side = step % 2
         if step > 0:
-            own_part(cur)
-
-        def far_part(d):
+            own_part()
+
+        def far_part(q, d):
             blocks(d, side).wait_recv()
             for r in range(REQ_CAP):
-                k = (d - 1) * REQ_CAP + r
+                k = q * REQ_CAP + r
                 link(k, dot(tile_of(BLK_DEV + k), inc[side, d - 1, r]))
 
-        each(far_part)
+        near_first(far_part)
         if step < STEPS - 1:
             def settle(i):
-                value = (total[i] + chain[meta[last_at + i]]) / deg[i]
+                value = (total[i] + chain[meta[last_at + i]]) * deg[i]
                 cur[i] = value.astype(jnp.bfloat16)
             by_four(settle)
             each(lambda d: blocks(d, side).wait_send())
@@ -195,7 +224,7 @@
             def finish(q, top):
                 for j in range(4):
                     i = q * 4 + j
-                    value = (total[i] + chain[meta[last_at + i]]) / deg[i]
+                    value = (total[i] + chain[meta[last_at + i]]) * deg[i]
                     total[i] = value
                     top = jnp.maximum(top, jnp.max(value.reshape(BS // 8, 8, -1), axis=0))
                 pltpu.make_async_copy(
@@ -240,16 +269,19 @@
     own = valid & (owner == me)
     same = (owner[:, None] == owner[None, :]) & remote[None, :] & (order[None, :] < order[:, None])
     rank = jnp.sum(same.astype(jnp.int32), axis=1)
-    k = jnp.where(remote, (jnp.mod(me - owner, n) - 1) * REQ_CAP + rank, -1)
+    d = jnp.mod(me - owner, n)
+    turn = (n - 2) - jnp.where(d > n // 2, 2 * (d - n // 2), jnp.maximum(n - 2 * d - 1, 0))
+    k = jnp.where(remote, turn * REQ_CAP + rank, -1)
+    asked = jnp.where(remote, (d - 1) * REQ_CAP + rank, -1)
     linked = (row[:, None] == row[None, :]) & remote[None, :] & (k[None, :] < k[:, None])
     prev = jnp.max(jnp.where(linked, k[None, :] + 1, 0), axis=1)
-    hit = k[:, None] == jnp.arange(links, dtype=jnp.int32)[None, :]
+    every = jnp.arange(links, dtype=jnp.int32)[None, :]
     mine = row[:, None] == jnp.arange(BLK_DEV, dtype=jnp.int32)[None, :]
     own_tile = jnp.sum(jnp.where(mine & own[:, None], order[:, None], 0), axis=0)
     last = jnp.max(jnp.where(mine & remote[:, None], k[:, None] + 1, 0), axis=0)
-    pick = lambda value: jnp.sum(jnp.where(hit, value[:, None], 0), axis=0)
-    meta = jnp.concatenate([own_tile, pick(order), pick(prev), last])
-    wanted = jnp.pad(pick(col_slot).reshape(n - 1, 1, REQ_CAP), ((0, 0), (0, 7), (0, 128 - REQ_CAP)))
+    pick = lambda at, value: jnp.sum(jnp.where(at[:, None] == every, value[:, None], 0), axis=0)
+    meta = jnp.concatenate([own_tile, pick(k, order), pick(k, prev), last])
+    wanted = jnp.pad(pick(asked, col_slot).reshape(n - 1, 1, REQ_CAP), ((0, 0), (0, 7), (0, 128 - REQ_CAP)))
     return meta, wanted
 
 
@@ -261,9 +293,10 @@
     slots = BLK_DEV + links
     parts = BS // affinity.shape[1]
     meta, wanted = plan(me, n, tile_rows, tile_cols, tile_count)
-    n_chunks = len(spans(0, BLK_DEV, 8)) + len(spans(BLK_DEV, slots, max(7, links // 4)))
+    n_chunks = len(tile_chunks(links))
     bf16, f32, i32 = jnp.bfloat16, jnp.float32, jnp.int32
     dma = pltpu.SemaphoreType.DMA
+    anywhere = pl.BlockSpec(memory_space=pl.ANY)
     vmem = pl.BlockSpec(memory_space=pltpu.VMEM)
     last, ratio = pl.pallas_call(
         functools.partial(kernel, n),
@@ -271,10 +304,11 @@
             jax.ShapeDtypeStruct((BLK_DEV, BS, genes), f32),
             jax.ShapeDtypeStruct((8, genes), f32),
         ),
-        in_specs=[pl.BlockSpec(memory_space=pltpu.SMEM), vmem, vmem, vmem],
-        out_specs=(pl.BlockSpec(memory_space=pl.ANY), vmem),
+        in_specs=[pl.BlockSpec(memory_space=pltpu.SMEM), vmem, anywhere, anywhere],
+        out_specs=(anywhere, vmem),
         scratch_shapes=[
             pltpu.VMEM((parts, slots, affinity.shape[1], BS), bf16),
+            pltpu.VMEM(affinity.shape, bf16),
             pltpu.VMEM((BLK_DEV, BS, genes), bf16),
             pltpu.VMEM((BLK_DEV, BS, genes), f32),
             pltpu.VMEM((BLK_DEV, BS, genes), f32),
@@ -287,7 +321,7 @@
             pltpu.VMEM((far, 16, genes), f32),
             dma((far,)), dma((far,)), dma((far,)), dma((2, far)),
             dma((n_chunks, 3)), dma((n_chunks, 3)), dma((far,)), dma((far,)),
-            dma, dma((BLK_DEV // 4,)),
+            dma, dma((2,)), dma((BLK_DEV // 4,)),
         ],
         compiler_params=pltpu.CompilerParams(
             collective_id=0, has_side_effects=True, vmem_limit_bytes=(62 if n > 8 else 48) * 2**20

time: 151 us -> 143 us (0.947)
  Pallas kernels: 140 us -> 133 us
    pallas_call x1, Pallas kernels: 140 us -> 133 us  [on_device(): pl.pallas_call(functools.partial(kernel, n), out_shape=(jax.ShapeDtypeStr...]
where the time goes in v2:
time: 143 us
  Pallas kernels  133 us (93%)
  other arithmetic  6.63 us (5%)
  local copies, waits for them, and re-layouts  3.18 us (2%)
    pallas_call x1, Pallas kernels, on_device(): pl.pallas_call(functools.partial(kernel, n), out_shape=(jax.ShapeDtypeStr...  133 us
    mul x1, other arithmetic, on_device(): return last.reshape(BLK_DEV * BS, genes) * ratio[0:1]  4.47 us
    unnamed x4, local copies, waits for them, and re-layouts  3.09 us

profile of v2, /device:TPU:0, one launch (start us, length us, event | category | flops | bytes accessed | tf_op | source)
XLA Modules:
  0.0 143.1 jit_solution(7354265768160538787)
XLA Ops:
  0.7 0.7 multiply_subtract_fusion
  1.3 0.2 convert_reduce_fusion
  1.5 0.1 select_reduce_fusion.3
  1.6 0.7 broadcast_add_fusion
  2.3 0.2 select_reduce_fusion
  2.5 0.1 select_reduce_fusion.2
  2.6 0.1 select_reduce_fusion.5
  2.7 0.1 pad_add_fusion.meta
  2.8 0.1 reshape.28
  2.9 0.0 copy-start
  2.9 1.6 %copy-done = bf16[8192,128]{1,0:T(8,128)(2,1)S(1)} copy-done((bf16[8192,128]{1,0:T(8,128)(2,1)S(1)}, bf16[8192,128]{1,0:T(8,128)(2,1)}, u32[]{:S(2)}) %copy-start) | copy-done | bytes 2097176
  4.5 0.0 copy-start.1
  4.5 1.5 %copy-done.1 = bf16[56,64,256]{2,1,0:T(8,128)(2,1)S(1)} copy-done((bf16[56,64,256]{2,1,0:T(8,128)(2,1)S(1)}, bf16[56,64,256]{2,1,0:T(8,128)(2,1)}, u32[]{:S(2)}) %copy-start.1) | copy-done | bytes 1835032
  6.0 132.6 %shard_map.55 = (f32[32,256,128]{2,1,0:T(8,128)}, f32[8,128]{1,0:T(8,128)S(1)}) custom-call(s32[106]{0:T(128)S(1)} %pad_add_fusion.meta, s32[7,8,128]{2,1,0:T(8,128)S(1)} %pad.4.wanted, bf16[32,256,128]{2,1,0:T(8,128)(2,1)S(1)} %bitcast.7, bf16[56,64,256]{2,1,0:T(8,128)(2,1)S(1)} %copy-done.1), custom_call_target="tpu_custom_call" | custom-call | tf_op jit(solution)/shard_map/pallas_call | solution.py:301
  138.6 4.5 %bitcast_multiply_fusion = f32[8192,128]{1,0:T(8,128)} fusion(f32[32,256,128]{2,1,0:T(8,128)} %get-tuple-element.7, f32[128]{0:T(128)S(1)} %slice_bitcast_fusion), kind=kLoop, calls=%fused_computation | loop fusion | flops 1048576 | bytes 8389120 | tf_op jit(solution)/shard_map/mul | solution.py:330
  (4 shorter events, 0.0 us)
Async XLA Ops:
  2.9 1.6 %copy-start = (bf16[8192,128]{1,0:T(8,128)(2,1)S(1)}, bf16[8192,128]{1,0:T(8,128)(2,1)}, u32[]{:S(2)}) copy-start(bf16[8192,128]{1,0:T(8,128)(2,1)} %param.5) | copy-start | bytes 6291460
  4.5 1.5 %copy-start.1 = (bf16[56,64,256]{2,1,0:T(8,128)(2,1)S(1)}, bf16[56,64,256]{2,1,0:T(8,128)(2,1)}, u32[]{:S(2)}) copy-start(bf16[56,64,256]{2,1,0:T(8,128)(2,1)} %aff_hbm.1) | copy-start | bytes 5505028

commit v3 on v2

--- a/solution.py
+++ b/solution.py
@@ -255,6 +255,10 @@
         return carry
 
     lax.fori_loop(0, BLK_DEV // 4, drain, 0)
+
+
+def rescale(ratio, last, scaled):
+    scaled[...] = last[...] * ratio[0:1]
 
 
 def plan(me, n, tile_rows, tile_cols, tile_count):
@@ -324,10 +328,21 @@
             dma, dma((2,)), dma((BLK_DEV // 4,)),
         ],
         compiler_params=pltpu.CompilerParams(
-            collective_id=0, has_side_effects=True, vmem_limit_bytes=(62 if n > 8 else 48) * 2**20
+            collective_id=0, has_side_effects=True, vmem_limit_bytes=62 * 2**20
         ),
     )(meta, wanted, expression.reshape(BLK_DEV, BS, genes), affinity)
-    return last.reshape(BLK_DEV * BS, genes) * ratio[0:1]
+    scaled = pl.pallas_call(
+        rescale,
+        grid=(8,),
+        out_shape=jax.ShapeDtypeStruct((BLK_DEV * BS, genes), f32),
+        in_specs=[
+            pl.BlockSpec((8, genes), lambda q: (0, 0)),
+            pl.BlockSpec((BLK_DEV * BS // 8, genes), lambda q: (q, 0)),
+        ],
+        out_specs=pl.BlockSpec((BLK_DEV * BS // 8, genes), lambda q: (q, 0)),
+        compiler_params=pltpu.CompilerParams(vmem_limit_bytes=32 * 2**20),
+    )(ratio, last.reshape(BLK_DEV * BS, genes))
+    return scaled
 
 
 def solution(mesh):

time: 143 us -> 144 us (level)
  other arithmetic: 6.63 us -> 2.7 us
  Pallas kernels: 133 us -> 136 us
    mul x1 -> x0, other arithmetic: 4.47 us -> none  [on_device(): return last.reshape(BLK_DEV * BS, genes) * ratio[0:1]]
    pallas_call x0 -> x1, Pallas kernels: none -> 3.48 us  [on_device(): pl.pallas_call(rescale, grid=(8,), out_shape=jax.ShapeDtypeStruct((BLK_DE...]
where the time goes in v3:
time: 144 us; the launch traced here: 143 us
  Pallas kernels  136 us (94%)
  local copies, waits for them, and re-layouts  3.57 us (2%)
  other arithmetic  2.7 us (2%)
    pallas_call x1, Pallas kernels, on_device(): pl.pallas_call(functools.partial(kernel, n), out_shape=(jax.ShapeDtypeStr...  133 us
    pallas_call x1, Pallas kernels, on_device(): pl.pallas_call(rescale, grid=(8,), out_shape=jax.ShapeDtypeStruct((BLK_DE...  3.48 us

profile of v3, /device:TPU:0, one launch (start us, length us, event | category | flops | bytes accessed | tf_op | source)
XLA Modules:
  0.0 143.4 jit_solution(1735587131559126225)
XLA Ops:
  0.7 0.7 multiply_subtract_fusion
  1.3 0.2 convert_reduce_fusion
  1.5 0.1 select_reduce_fusion.3
  1.6 0.7 broadcast_add_fusion
  2.3 0.2 select_reduce_fusion
  2.5 0.1 select_reduce_fusion.2
  2.6 0.1 select_reduce_fusion.5
  2.7 0.6 pad_add_fusion.meta
  3.4 0.1 reshape.28
  3.5 0.6 pad.4.wanted
  4.1 133.0 %shard_map.55 = (f32[32,256,128]{2,1,0:T(8,128)}, f32[8,128]{1,0:T(8,128)}) custom-call(s32[106]{0:T(128)} %pad_add_fusion.meta, s32[7,8,128]{2,1,0:T(8,128)} %pad.4.wanted, bf16[32,256,128]{2,1,0:T(8,128)(2,1)} %bitcast.5, bf16[56,64,256]{2,1,0:T(8,128)(2,1)} %aff_hbm.1), custom_call_target="tpu_custom_call" | custom-call | tf_op jit(solution)/shard_map/pallas_call | solution.py:305
  137.1 0.0 copy-start
  137.1 2.2 %copy-done = f32[32,256,128]{2,1,0:T(8,128)S(1)} copy-done((f32[32,256,128]{2,1,0:T(8,128)S(1)}, f32[32,256,128]{2,1,0:T(8,128)}, u32[]{:S(2)}) %copy-start) | copy-done | bytes 4194328
  139.3 0.0 copy-start.1
  139.3 0.7 copy-done.1
  140.0 3.5 %shard_map.56 = f32[8192,128]{1,0:T(8,128)} custom-call(f32[8,128]{1,0:T(8,128)S(1)} %copy-done.1, f32[8192,128]{1,0:T(8,128)S(1)} %bitcast.4), custom_call_target="tpu_custom_call" | custom-call | tf_op jit(solution)/shard_map/pallas_call | solution.py:334
  (2 shorter events, 0.0 us)
Async XLA Ops:
  137.1 2.2 %copy-start = (f32[32,256,128]{2,1,0:T(8,128)S(1)}, f32[32,256,128]{2,1,0:T(8,128)}, u32[]{:S(2)}) copy-start(f32[32,256,128]{2,1,0:T(8,128)} %get-tuple-element.8) | copy-start | bytes 12582916
  139.3 0.7 copy-start.1

commit v4 on v3

--- a/solution.py
+++ b/solution.py
@@ -340,7 +340,7 @@
             pl.BlockSpec((BLK_DEV * BS // 8, genes), lambda q: (q, 0)),
         ],
         out_specs=pl.BlockSpec((BLK_DEV * BS // 8, genes), lambda q: (q, 0)),
-        compiler_params=pltpu.CompilerParams(vmem_limit_bytes=32 * 2**20),
+        compiler_params=pltpu.CompilerParams(vmem_limit_bytes=62 * 2**20),
     )(ratio, last.reshape(BLK_DEV * BS, genes))
     return scaled
 

time: 144 us -> 144 us (level)
  Pallas kernels: 136 us -> 140 us
  local copies, waits for them, and re-layouts: 3.57 us -> 0.7 us
    pallas_call x1, Pallas kernels: 3.48 us -> 6.6 us  [on_device(): pl.pallas_call(rescale, grid=(8,), out_shape=jax.ShapeDtypeStruct((BLK_DE...]
    unnamed x4 -> x0, local copies, waits for them, and re-layouts: 2.87 us -> none
where the time goes in v4:
time: 144 us
  Pallas kernels  140 us (97%)
  other arithmetic  2.7 us (2%)
    pallas_call x1, Pallas kernels, on_device(): pl.pallas_call(functools.partial(kernel, n), out_shape=(jax.ShapeDtypeStr...  133 us
    pallas_call x1, Pallas kernels, on_device(): pl.pallas_call(rescale, grid=(8,), out_shape=jax.ShapeDtypeStruct((BLK_DE...  6.6 us

profile of v4, /device:TPU:0, one launch (start us, length us, event | category | flops | bytes accessed | tf_op | source)
XLA Modules:
  0.0 143.7 jit_solution(4543466786825462948)
XLA Ops:
  0.7 0.7 multiply_subtract_fusion
  1.3 0.2 convert_reduce_fusion
  1.5 0.1 select_reduce_fusion.3
  1.6 0.7 broadcast_add_fusion
  2.3 0.2 select_reduce_fusion
  2.5 0.1 select_reduce_fusion.2
  2.6 0.1 select_reduce_fusion.5
  2.7 0.6 pad_add_fusion.meta
  3.4 0.1 reshape.28
  3.5 0.6 pad.4.wanted
  4.1 133.0 %shard_map.55 = (f32[32,256,128]{2,1,0:T(8,128)}, f32[8,128]{1,0:T(8,128)}) custom-call(s32[106]{0:T(128)} %pad_add_fusion.meta, s32[7,8,128]{2,1,0:T(8,128)} %pad.4.wanted, bf16[32,256,128]{2,1,0:T(8,128)(2,1)} %bitcast.5, bf16[56,64,256]{2,1,0:T(8,128)(2,1)} %aff_hbm.1), custom_call_target="tpu_custom_call" | custom-call | tf_op jit(solution)/shard_map/pallas_call | solution.py:305
  137.1 6.6 %shard_map.56 = f32[8192,128]{1,0:T(8,128)} custom-call(f32[8,128]{1,0:T(8,128)} %get-tuple-element.7.ratio, f32[8192,128]{1,0:T(8,128)} %bitcast.4), custom_call_target="tpu_custom_call" | custom-call | tf_op jit(solution)/shard_map/pallas_call | solution.py:334
  (2 shorter events, 0.0 us)
